TPU v7x, 256 devices: a whole 4x4x8 slice. The times are simulated.
256 devices in a mesh: prow: 8 (over y, core), pcol: 32 (over z, x).
Axes of the slice: x: 4, y: 4, z: 8, core: 2. Of those that a mesh axis runs over, the one named last changes fastest.
Arguments:
- matrix: float32 [4096, 16384], P('prow', 'pcol'), may hold values from -6 to 6
- pivots_first: int32 [512], replicated, may hold values from 512 to 4095, as said below
- pivots_second: int32 [512], replicated, may hold values from 1024 to 4095, as said below
- lower_first: float32 [512, 512], replicated, as said below
- upper_first: float32 [512, 512], replicated, as said below
- lower_second: float32 [512, 512], replicated, as said below
- upper_second: float32 [512, 512], replicated, as said below
Outputs:
- factored: float32 [4096, 16384], P('prow', 'pcol')
Inputs may be any that keep to these rules, and one draw needn't show every extreme that they name: `pivots_first`: 512 distinct working-order row indices; both the smallest and the largest allowed value occur. `pivots_second`: 512 distinct working-order row indices; both the smallest and the largest allowed value occur. `lower_first`: unit lower triangular. `upper_first`: upper triangular with a positive diagonal. `lower_second`: unit lower triangular. `upper_second`: upper triangular with a positive diagonal.
All inputs are finite; a program needn't handle non-finite values.
Results may differ from a plain program's by a relative error of at most 0.00009.
Values sent between devices are 32-bit elements; how exact they have to be, the bound alone decides.
A program may use at most 64 MiB of HBM per device.

v0:
```python
import jax
import jax.numpy as jnp
from jax import lax
from jax.sharding import PartitionSpec as P


def from_root(shard, axis, root):
    mine = lax.axis_index(axis) == root
    return lax.psum(jnp.where(mine, shard, jnp.zeros_like(shard)), axis)


def product(left, right):
    return jnp.dot(left, right, precision=lax.Precision.HIGHEST, preferred_element_type=jnp.float32)


def locate(pivots, block, nprow, prow_index):
    pivot_block = pivots // block
    pivot_owner = pivot_block % nprow
    pivot_local = pivot_block // nprow * block + pivots % block
    return (pivot_owner == prow_index, pivot_local)


def place_rows(target_rows, old_top, new_top, owned, pivot_local, top_owner, prow_index):
    rows_local = target_rows.shape[0]
    target = jnp.where(owned, pivot_local, rows_local)
    target_rows = target_rows.at[target].set(old_top, mode="drop")
    placed_top = jnp.where(prow_index == top_owner, new_top, target_rows)
    return placed_top


def eliminate(work, pivots, lower, upper, step, context):
    nprow, npcol, prow_index, pcol_index, row_global, col_global = context
    block = lower.shape[0]
    top_owner = step % nprow
    panel_owner = step % npcol
    panel_local = step // npcol * block
    edge = (step + 1) * block
    top_source = work
    old_top = from_root(top_source, "prow", top_owner)
    owned, pivot_local = locate(pivots, block, nprow, prow_index)
    picked_source = work[pivot_local]
    picked = jnp.where(owned[:, None], picked_source, 0.0)
    trailing_cols = col_global >= edge
    new_top = lax.psum(picked, "prow")
    solved = product(lower, new_top)
    new_top = jnp.where(trailing_cols[None, :], solved, new_top)
    work = place_rows(work, old_top, new_top, owned, pivot_local, top_owner, prow_index)
    panel = from_root(work, "pcol", panel_owner)
    factor = product(panel, upper)
    trailing_rows = row_global >= edge
    factor_used = jnp.where(trailing_rows[:, None], factor, 0.0)
    urows_used = jnp.where(trailing_cols[None, :], new_top, 0.0)
    return (work, factor, factor_used, urows_used, trailing_rows, panel_owner, panel_local)


def apply_update(state, pcol_index):
    work, factor, factor_used, urows_used, trailing_rows, panel_owner, panel_local = state
    work = work - product(factor_used, urows_used)
    keep_factor = jnp.logical_and(trailing_rows[:, None], pcol_index == panel_owner)
    placed_panel = jnp.where(keep_factor, factor, work)
    return placed_panel


def on_device(
    matrix, pivots_first, pivots_second, lower_first, upper_first, lower_second, upper_second
):
    nprow = lax.axis_size("prow")
    npcol = lax.axis_size("pcol")
    prow_index = lax.axis_index("prow")
    pcol_index = lax.axis_index("pcol")
    block = lower_first.shape[0]
    rows_local, cols_local = matrix.shape
    row_iota = jnp.arange(rows_local, dtype=jnp.int32)
    col_iota = jnp.arange(cols_local, dtype=jnp.int32)
    row_global = (row_iota // block * nprow + prow_index) * block + row_iota % block
    col_global = (col_iota // block * npcol + pcol_index) * block + col_iota % block
    context = (nprow, npcol, prow_index, pcol_index, row_global, col_global)
    state = eliminate(matrix, pivots_first, lower_first, upper_first, 0, context)
    work = apply_update(state, pcol_index)
    state = eliminate(work, pivots_second, lower_second, upper_second, 1, context)
    return apply_update(state, pcol_index)


def solution(mesh):
    placed = (P("prow", "pcol"), P(), P(), P(), P(), P(), P())
    return jax.shard_map(
        on_device, mesh=mesh, in_specs=placed, out_specs=P("prow", "pcol"), check_vma=False
    )
```

profile of v0, /device:TPU:40, one launch (start us, length us, event | category | flops | bytes accessed | tf_op | source)
XLA Modules:
  0.0 501.7 jit_solution(7744166941727522942)
XLA Ops:
  6.5 1.3 copy.50
  7.9 0.7 copy-done.3
  8.6 0.3 copy.22
  8.9 2.3 gather_fusion
  11.3 2.5 copy.21
  13.8 2.8 broadcast_select_fusion.4
  16.6 0.0 all-reduce.13.cloned.1.call-update
  16.6 0.0 all-reduce.7.cloned.1.call-start
  16.7 71.1 %all-reduce.13.cloned.1.call-done = (f32[512,512]{0,1:T(8,128)}, f32[512,512]{0,1:T(8,128)}) async-done(((f32[512,512]{0,1:T(8,128)}, f32[512,512]{0,1:T(8,128)}), (f32[512,512]{0,1:T(8,128)}, f32[512,512]{0,1:T(8,128)})) %all-reduce.13.cloned.1.call-update) | async-done | bytes 2097168 | tf_op jit(solution)/shard_map/psum | solution.py:44
  87.8 1.6 copy.23
  89.3 2.7 scatter_fusion
  92.0 0.3 copy.24
  92.3 4.4 broadcast_select_fusion.3
  96.8 0.0 all-reduce.11.cloned.1.call-start
  96.9 0.6 copy-done.4
  97.5 149.9 %all-reduce.7.cloned.1.call-done = f32[512,512]{0,1:T(8,128)} async-done(((f32[512,512]{0,1:T(8,128)}), f32[512,512]{0,1:T(8,128)}) %all-reduce.7.cloned.1.call-update) | async-done | bytes 1048592 | tf_op jit(solution)/shard_map/psum | solution.py:9
  247.4 3.4 fusion.45
  250.8 3.4 broadcast_select_fusion.1
  254.2 1.6 copy.28
  255.8 1.6 gather_fusion.1
  257.4 1.3 copy.29
  258.7 2.3 broadcast_select_fusion.2
  261.0 0.0 all-reduce.9.cloned.1.call-start
  261.1 66.9 %all-reduce.11.cloned.1.call-done = (f32[512,512]{0,1:T(8,128)}, f32[512,512]{0,1:T(8,128)}) async-done(((f32[512,512]{0,1:T(8,128)}, f32[512,512]{0,1:T(8,128)}), (f32[512,512]{0,1:T(8,128)}, f32[512,512]{0,1:T(8,128)})) %all-reduce.11.cloned.1.call-update) | async-done | bytes 2097168 | tf_op jit(solution)/shard_map/psum | solution.py:44
  328.1 1.6 copy.31
  329.6 2.8 scatter_fusion.1
  332.5 0.3 copy.32
  332.8 5.1 %broadcast_select_fusion = (f32[512,512]{0,1:T(8,128)}, f32[512,512]{0,1:T(8,128)}) fusion(f32[512,512]{0,1:T(8,128)S(1)} %copy.32, pred[]{:T(512)S(6)} %eq.32, pred[]{:T(512)S(6)} %eq.31, f32[512,512]{0,1:T(8,128)} %get-tuple-element.5, f32[512,512]{1,0:T(8,128)} %param.12, pred[512]{0:T(512)(128)(4,1)S(1)} %broadcast_compare_fusion), kind=kOutput, calls=%fused_computation.16 | convolution fusion | flops 1611399168 | bytes 5243394 | tf_op jit(solution)/shard_map/dot_general | solution.py:13
  338.0 150.6 %all-reduce.9.cloned.1.call-done = f32[512,512]{0,1:T(8,128)} async-done(((f32[512,512]{0,1:T(8,128)}), f32[512,512]{0,1:T(8,128)}) %all-reduce.9.cloned.1.call-update) | async-done | bytes 1048592 | tf_op jit(solution)/shard_map/psum | solution.py:9
  488.6 3.2 fusion.46
  491.8 2.1 fusion
  493.9 1.3 copy.36
  (23 shorter events, 0.2 us)
Async XLA Ops:
  6.5 85.8 %copy-start = (f32[512,512]{1,0:T(8,128)S(1)}, f32[512,512]{1,0:T(8,128)}, u32[]{:S(2)}) copy-start(f32[512,512]{1,0:T(8,128)} %param.10) | copy-start | bytes 3145732
  6.5 81.2 %all-reduce.13.cloned.1.call-start = ((), (), s32[]{:S(2)}) async-start(), calls=%async_computation.3 | async-start | bytes 4194304 | tf_op jit(solution)/shard_map/psum | solution.py:44
  7.9 0.7 copy-start.3
  16.6 230.8 %all-reduce.7.cloned.1.call-start = ((), (), s32[]{:S(2)}) async-start(), calls=%async_computation | async-start | bytes 2097152 | tf_op jit(solution)/shard_map/psum | solution.py:9
  96.8 0.7 copy-start.4
  96.8 231.2 %all-reduce.11.cloned.1.call-start = ((), (), s32[]{:S(2)}) async-start(), calls=%async_computation.2 | async-start | bytes 4194304 | tf_op jit(solution)/shard_map/psum | solution.py:44
  261.0 227.5 %all-reduce.9.cloned.1.call-start = ((), (), s32[]{:S(2)}) async-start(), calls=%async_computation.1 | async-start | bytes 2097152 | tf_op jit(solution)/shard_map/psum | solution.py:9
  337.9 150.7 %copy-start.2 = (f32[512,512]{1,0:T(8,128)S(1)}, f32[512,512]{1,0:T(8,128)}, u32[]{:S(2)}) copy-start(f32[512,512]{1,0:T(8,128)} %param.13) | copy-start | bytes 3145732
  488.6 3.2 copy-start.1
Sparse Core Ops, SparseCore 0:
  16.7 70.9 all-reduce.12
  96.9 150.4 all-reduce.6
  261.2 66.8 all-reduce.10
  338.0 150.4 all-reduce.8
where the time goes:
time: 504 us; the launch traced here: 502 us
  waiting for transfers between devices  439 us (87%)
  local copies, waits for them, and re-layouts  22.9 us (5%)
  matrix products  21.6 us (4%)
  between operations  13.3 us (3%)
  other arithmetic  5.22 us (1%)
    psum x2, waiting for transfers between devices, from_root(): return lax.psum(jnp.where(mine, shard, jnp.zeros_like(shard)), axis)  300 us
    psum x2, waiting for transfers between devices, eliminate(): new_top = lax.psum(picked, 'prow')  138 us
    dot_general x6, matrix products, product(): jnp.dot(left, right, precision=lax.Precision.HIGHEST, preferred_element_t...  21.6 us
  transfers between devices with their start and end apart: 4, of which 4 were waited for; matrix products, arithmetic and copies ran while one was open for 0% of the time, Pallas kernels for 0%

commit v1 on v0

v1 whole, which is shorter than its diff:
```python
import functools

import jax
import jax.numpy as jnp
from jax import lax
from jax.experimental import pallas as pl
from jax.experimental.pallas import tpu as pltpu
from jax.sharding import PartitionSpec as P

MESH = pl.DeviceIdType.MESH
NB = 512
HALF = NB // 2
NY, NC, NZ, NX = 4, 2, 8, 4
PART = NB // NX
SUBS = 2
SUB = PART // SUBS
WCH = 4
WROWS = HALF // WCH
F32 = jnp.float32
BF16 = jnp.bfloat16


def dot1(a, b):
    return jnp.dot(a, b, preferred_element_type=F32)


def split2(a):
    high = a.astype(BF16)
    return high, (a - high.astype(F32)).astype(BF16)


def split3(a):
    high = a.astype(BF16)
    rest = a - high.astype(F32)
    mid = rest.astype(BF16)
    return high, mid, (rest - mid.astype(F32)).astype(BF16)


def product(a, b):
    ah, al = split2(a)
    bh, bl = split2(b)
    return dot1(ah, bh) + (dot1(ah, bl) + dot1(al, bh))


def pick(onehot, parts):
    high, mid, low = parts
    return dot1(onehot, high) + (dot1(onehot, mid) + dot1(onehot, low))


def onehot_of(source, first):
    lanes = lax.broadcasted_iota(jnp.int32, (NB, NB), 1).astype(F32) + first
    return jnp.where(source == lanes, 1.0, 0.0).astype(BF16)


def kernel(
    w_ref, pf_ref, ps_ref, l0_hbm, u0_hbm, l1_hbm, u1_hbm, out_ref,
    l0, u0, l1, u1, xp, sib, hs, rsr, xf, wb, xi, px0, px1, c10, c01, li0, ur0, f1,
    fac_sem, sib_s, sib_r, w_s, w_r, ws_s, ws_r, rs_s, rs_r, ag_s, ag_r, as_s, as_r,
    a_s, a_r, b_s, b_r, c_s, c_r, cs_s, cs_r,
):
    prow = lax.axis_index("prow")
    pcol = lax.axis_index("pcol")
    y, h = prow // 2, prow % 2
    z, x = pcol // NX, pcol % NX
    other = 1 - h

    def at(dy=0, dc=0, dz=0, dx=0):
        return {
            "prow": ((y + dy + NY) % NY) * NC + (h + dc) % NC,
            "pcol": ((z + dz + NZ) % NZ) * NX + (x + dx + NX) % NX,
        }

    sibling = at(dc=1)
    pending = []

    def when(cond, fn):
        if cond is None:
            fn()
        else:
            pl.when(cond)(fn)

    def send(src, dst, ssem, rsem, device, cond=None):
        copy = pltpu.make_async_remote_copy(
            src_ref=src, dst_ref=dst, send_sem=ssem, recv_sem=rsem, device_id=device, device_id_type=MESH
        )
        when(cond, copy.start)
        pending.append((cond, copy))

    def await_recv(dst, ssem, rsem, cond=None):
        copy = pltpu.make_async_remote_copy(
            src_ref=dst, dst_ref=dst, send_sem=ssem, recv_sem=rsem, device_id=sibling, device_id_type=MESH
        )
        when(cond, copy.wait_recv)

    factors = [
        pltpu.make_async_copy(src, dst, fac_sem.at[k])
        for k, (src, dst) in enumerate(((l0_hbm, l0), (u0_hbm, u0), (l1_hbm, l1), (u1_hbm, u1)))
    ]
    for copy in factors:
        copy.start()

    partners = [
        at(dc=1), at(dy=1), at(dy=2), at(dy=3), at(dx=1), at(dx=2), at(dx=3),
        at(dz=1), at(dz=2), at(dz=-1), at(dz=-2),
    ]
    barrier = pltpu.get_barrier_semaphore()
    for partner in partners:
        pl.semaphore_signal(barrier, inc=1, device_id=partner, device_id_type=MESH)
    pl.semaphore_wait(barrier, len(partners))

    top = y == 0

    def wslice(way, k):
        return wb.at[h, pl.ds(way * HALF + k * WROWS, WROWS)]

    for k in range(WCH):
        for way, dy in ((0, 1), (1, -1)):
            rows = pl.ds(way * HALF + k * WROWS, WROWS)
            send(w_ref.at[rows], wslice(way, k), w_s.at[way, k], w_r.at[way, k], at(dy=dy), top)

    base = (prow * NB).astype(F32)
    pf_row = pf_ref[...].astype(F32)
    ps_row = ps_ref[...].astype(F32)
    row_id = lax.broadcasted_iota(jnp.int32, (NB, NB), 0).astype(F32)
    col_id = lax.broadcasted_iota(jnp.int32, (NB, NB), 1).astype(F32)
    diagonal = row_id == col_id
    pf_col = jnp.sum(jnp.where(diagonal, pf_row, 0.0), axis=1, keepdims=True)
    ps_col = jnp.sum(jnp.where(diagonal, ps_row, 0.0), axis=1, keepdims=True)
    chained = jnp.sum(jnp.where(ps_col == pf_row, col_id + 1.0, 0.0), axis=1, keepdims=True)
    src1 = jnp.where(chained > 0.0, chained - 1.0, ps_col)

    w_parts = split3(w_ref[...])
    xp[0:NB] = pick(onehot_of(pf_col, base), w_parts)
    far = pl.multiple_of(other * HALF, HALF)
    near = pl.multiple_of(h * HALF, HALF)
    send(xp.at[0:NB, pl.ds(far, HALF)], sib.at[0:NB], sib_s.at[0], sib_r.at[0], sibling)
    xp[NB:] = pick(onehot_of(src1, base), w_parts)
    send(xp.at[NB:, pl.ds(far, HALF)], sib.at[NB:], sib_s.at[1], sib_r.at[1], sibling)

    for k in range(2):
        rows = pl.ds(k * NB, NB)
        await_recv(sib.at[rows], sib_s.at[k], sib_r.at[k])
        hs[rows] = xp[rows, pl.ds(near, HALF)] + sib[rows]

    def chunk(c):
        return pl.ds(pl.multiple_of(c * HALF, HALF), HALF)

    for d in range(1, NY):
        send(hs.at[chunk((y + d) % NY)], rsr.at[d - 1], rs_s.at[d - 1], rs_r.at[d - 1], at(dy=d))

    def relay_all(order):
        for way, k in order:
            ref = wslice(way, k)
            await_recv(ref, w_s.at[way, k], w_r.at[way, k])
            hop = y if way == 0 else NY - y
            onward = pltpu.make_async_remote_copy(
                src_ref=ref, dst_ref=ref, send_sem=w_s.at[way, k], recv_sem=w_r.at[way, k],
                device_id=at(dy=1 - 2 * way), device_id_type=MESH,
            )
            pl.when(hop < NY - 1)(onward.start)
            pltpu.make_async_remote_copy(
                src_ref=ref, dst_ref=ref, send_sem=ws_s.at[way, k], recv_sem=ws_r.at[way, k],
                device_id=sibling, device_id_type=MESH,
            ).start()

    first = [(0, k) for k in range(WCH)]
    second = [(1, k) for k in range(WCH)]
    mixed = [(way, k) for k in range(WCH) for way in range(2)]
    pl.when(y == 1)(lambda: relay_all(first + second))
    pl.when(y == 2)(lambda: relay_all(mixed))
    pl.when(y == 3)(lambda: relay_all(second + first))
    below = y > 0
    for way, k in mixed:
        ref = wslice(way, k)
        hop = y if way == 0 else NY - y
        onward = pltpu.make_async_remote_copy(
            src_ref=ref, dst_ref=ref, send_sem=w_s.at[way, k], recv_sem=w_r.at[way, k],
            device_id=at(dy=1 - 2 * way), device_id_type=MESH,
        )
        pending.append((jnp.logical_and(below, hop < NY - 1), onward))
        across = pltpu.make_async_remote_copy(
            src_ref=ref, dst_ref=ref, send_sem=ws_s.at[way, k], recv_sem=ws_r.at[way, k],
            device_id=sibling, device_id_type=MESH,
        )
        pending.append((below, across))

    mine = chunk(y)
    for d in range(1, NY):
        await_recv(rsr.at[d - 1], rs_s.at[d - 1], rs_r.at[d - 1])
    xf[h, mine] = (hs[mine] + rsr[0]) + (rsr[1] + rsr[2])
    for d in range(1, NY):
        send(xf.at[h, mine], xf.at[h, mine], ag_s.at[d - 1], ag_r.at[d - 1], at(dy=d))
    send(xf.at[h, mine], xf.at[h, mine], as_s.at[0], as_r.at[0], sibling)

    def place_rows():
        for way, k in mixed:
            ref = wb.at[other, pl.ds(way * HALF + k * WROWS, WROWS)]
            await_recv(ref, ws_s.at[way, k], ws_r.at[way, k])
        here = base + row_id[:, 0:1]
        moved = jnp.sum(jnp.where(pf_row == here, col_id + 1.0, 0.0), axis=1, keepdims=True)
        under = col_id + float(NB)
        linked = jnp.sum(jnp.where(pf_col == under, row_id + 1.0, 0.0), axis=0, keepdims=True)
        origin = jnp.where(linked > 0.0, linked, under[0:1] + 1.0)
        taken = jnp.sum(jnp.where(ps_row == here, origin, 0.0), axis=1, keepdims=True)
        source = jnp.where(taken > 0.0, taken, moved) - 1.0
        incoming = pick(onehot_of(source, 0.0), split3(wb[0]))
        incoming += pick(onehot_of(source, float(NB)), split3(wb[1]))
        xi[...] = jnp.where(source < 0.0, w_ref[...], incoming)

    pl.when(below)(place_rows)

    def keep_panel(panel):
        panel[...] = xi[...]

    pl.when(jnp.logical_and(below, pcol == 0))(lambda: keep_panel(px0))
    pl.when(jnp.logical_and(below, pcol == 1))(lambda: keep_panel(px1))

    units = [(b, s) for b in range(4) for s in range(SUBS)]

    def rows_of(unit, part):
        b, s = unit
        rows = pl.ds(pl.multiple_of(part * PART + s * SUB, SUB), SUB)
        return (px0.at[rows], px1.at[rows], c10.at[h, rows], c01.at[h, rows])[b]

    def both(*conds):
        conds = [c for c in conds if c is not None]
        return functools.reduce(jnp.logical_and, conds) if conds else None

    row0 = z == 0

    def scatter_parts(chosen):
        for u, unit in chosen:
            root = unit[0] % 2
            plane = below if unit[0] < 2 else None
            for d in range(1, NX):
                ref = rows_of(unit, (root + d) % NX)
                send(ref, ref, a_s.at[u, d - 1], a_r.at[u], at(dx=d), both(plane, pcol == root))

    def spread(chosen):
        for u, unit in chosen:
            root = unit[0] % 2
            plane = below if unit[0] < 2 else None
            ref = rows_of(unit, x)
            await_recv(ref, a_s.at[u, 0], a_r.at[u], both(plane, row0, x != root))
            await_recv(ref, b_s.at[u, 0], b_r.at[u], both(plane, z != 0))
            up = both(plane, jnp.logical_or(row0, z == 2))
            down = both(plane, jnp.logical_or(row0, z == 6))
            send(ref, ref, b_s.at[u, 0], b_r.at[u], at(dz=1), up)
            send(ref, ref, b_s.at[u, 1], b_r.at[u], at(dz=2), up)
            send(ref, ref, b_s.at[u, 2], b_r.at[u], at(dz=-1), down)
            send(ref, ref, b_s.at[u, 3], b_r.at[u], at(dz=-2), both(plane, row0))
            for d in range(1, NX):
                needed = jnp.logical_not(jnp.logical_and(row0, (x + d) % NX == root))
                send(ref, ref, c_s.at[u, d - 1], c_r.at[u, d - 1], at(dx=d), both(plane, needed))

    def gather(chosen):
        for u, unit in chosen:
            root = unit[0] % 2
            plane = below if unit[0] < 2 else None
            needed = jnp.logical_not(pcol == root)
            for d in range(1, NX):
                ref = rows_of(unit, (x - d + NX) % NX)
                await_recv(ref, c_s.at[u, d - 1], c_r.at[u, d - 1], both(plane, needed))

    panels = [(u, unit) for u, unit in enumerate(units) if unit[0] < 2]
    corners = [(u, unit) for u, unit in enumerate(units) if unit[0] >= 2]

    scatter_parts(panels)
    spread(panels)

    for d in range(1, NY):
        part = xf.at[h, chunk((y - d + NY) % NY)]
        await_recv(part, ag_s.at[d - 1], ag_r.at[d - 1])
        send(part, part, as_s.at[d], as_r.at[d], sibling)

    def keep_corner(corner, first_row):
        corner[h] = xf[h, first_row:first_row + NB]

    pl.when(pcol == 0)(lambda: keep_corner(c10, NB))
    pl.when(pcol == 1)(lambda: keep_corner(c01, 0))
    scatter_parts(corners)
    spread(corners)

    for d in range(NY):
        part = xf.at[other, chunk((y - d + NY) % NY)]
        await_recv(part, as_s.at[d], as_r.at[d])
    for copy in factors:
        copy.wait()

    def halves(ref, rows):
        return jnp.concatenate([ref[0, rows], ref[1, rows]], axis=1)

    ur0[...] = product(l0[...], halves(xf, pl.ds(0, NB)))

    gather(panels)

    def early():
        li0[...] = product(px0[...], u0[...])
        f1[...] = xi[...] - product(li0[...], ur0[...])

    pl.when(below)(early)

    gather(corners)
    for b, corner in ((0, c10), (1, c01)):
        send(corner.at[h], corner.at[h], cs_s.at[b], cs_r.at[b], sibling)
    for b, corner in ((0, c10), (1, c01)):
        await_recv(corner.at[other], cs_s.at[b], cs_r.at[b])

    def first_block():
        @pl.when(pcol == 0)
        def _():
            out_ref[...] = halves(xf, pl.ds(0, NB))

        @pl.when(pcol > 0)
        def _():
            out_ref[...] = ur0[...]

    def other_blocks():
        whole = pl.ds(0, NB)
        lower10 = product(halves(c10, whole), u0[...])

        @pl.when(jnp.logical_and(top, pcol == 0))
        def _():
            out_ref[...] = lower10

        @pl.when(jnp.logical_not(jnp.logical_and(top, pcol == 0)))
        def _():
            second = halves(xf, pl.ds(NB, NB)) - product(lower10, ur0[...])

            @pl.when(jnp.logical_and(top, pcol == 1))
            def _():
                out_ref[...] = second

            @pl.when(jnp.logical_and(top, pcol > 1))
            def _():
                out_ref[...] = product(l1[...], second)

            @pl.when(below)
            def _():
                urow = product(l1[...], second)
                upper01 = product(l0[...], halves(c01, whole))
                lower1 = product(px1[...] - product(li0[...], upper01), u1[...])

                @pl.when(pcol == 0)
                def _():
                    out_ref[...] = li0[...]

                @pl.when(pcol == 1)
                def _():
                    out_ref[...] = lower1

                @pl.when(pcol > 1)
                def _():
                    out_ref[...] = f1[...] - product(lower1, urow)

    pl.when(prow == 0)(first_block)
    pl.when(prow > 0)(other_blocks)

    for cond, copy in pending:
        when(cond, copy.wait_send)


def on_device(
    matrix, pivots_first, pivots_second, lower_first, upper_first, lower_second, upper_second
):
    vmem = pl.BlockSpec(memory_space=pltpu.VMEM)
    anywhere = pl.BlockSpec(memory_space=pl.ANY)
    block = (NB, NB)
    dma = pltpu.SemaphoreType.DMA
    nu = 4 * SUBS
    return pl.pallas_call(
        kernel,
        out_shape=jax.ShapeDtypeStruct(block, F32),
        in_specs=[vmem] * 3 + [anywhere] * 4,
        out_specs=vmem,
        scratch_shapes=[pltpu.VMEM(block, F32)] * 4
        + [
            pltpu.VMEM((2 * NB, NB), F32),
            pltpu.VMEM((2 * NB, HALF), F32),
            pltpu.VMEM((2 * NB, HALF), F32),
            pltpu.VMEM((NY - 1, HALF, HALF), F32),
            pltpu.VMEM((2, 2 * NB, HALF), F32),
            pltpu.VMEM((2, NB, NB), F32),
            pltpu.VMEM(block, F32),
            pltpu.VMEM(block, F32),
            pltpu.VMEM(block, F32),
            pltpu.VMEM((2, NB, HALF), F32),
            pltpu.VMEM((2, NB, HALF), F32),
            pltpu.VMEM(block, F32),
            pltpu.VMEM(block, F32),
            pltpu.VMEM(block, F32),
        ]
        + [
            dma((4,)),
            dma((2,)), dma((2,)),
            dma((2, WCH)), dma((2, WCH)),
            dma((2, WCH)), dma((2, WCH)),
            dma((NY - 1,)), dma((NY - 1,)),
            dma((NY - 1,)), dma((NY - 1,)),
            dma((NY,)), dma((NY,)),
            dma((nu, NX - 1)), dma((nu,)),
            dma((nu, 4)), dma((nu,)),
            dma((nu, NX - 1)), dma((nu, NX - 1)),
            dma((2,)), dma((2,)),
        ],
        compiler_params=pltpu.CompilerParams(
            collective_id=0, has_side_effects=True, vmem_limit_bytes=56 << 20
        ),
    )(
        matrix, pivots_first.reshape(1, NB), pivots_second.reshape(1, NB),
        lower_first, upper_first, lower_second, upper_second,
    )


def solution(mesh):
    placed = (P("prow", "pcol"), P(), P(), P(), P(), P(), P())
    return jax.shard_map(
        on_device, mesh=mesh, in_specs=placed, out_specs=P("prow", "pcol"), check_vma=False
    )
```

time: 504 us -> 126 us (0.25)
  the two profiles are of different devices: /device:TPU:40 before, /device:TPU:139 now
where the time goes in v1:
time: 126 us; the launch traced here: 125 us
  Pallas kernels  123 us (98%)
  local copies, waits for them, and re-layouts  2.26 us (2%)
    pallas_call x1, Pallas kernels, on_device(): pl.pallas_call(kernel, out_shape=jax.ShapeDtypeStruct(block, F32), in_spe...  123 us

profile of v1, /device:TPU:139, one launch (start us, length us, event | category | flops | bytes accessed | tf_op | source)
XLA Modules:
  0.0 125.5 jit_solution(16164756323298562798)
XLA Ops:
  0.0 123.2 %shard_map.73 = f32[512,512]{1,0:T(8,128)} custom-call(f32[512,512]{1,0:T(8,128)} %w_ref.1, s32[1,512]{1,0:T(1,128)} %bitcast.2, s32[1,512]{1,0:T(1,128)} %bitcast.3, f32[512,512]{1,0:T(8,128)} %l0_hbm.1, f32[512,512]{1,0:T(8,128)} %u0_hbm.1, f32[512,512]{1,0:T(8,128)} %l1_hbm.1, f32[512,512]{1,0:T(8,128)} %u1_hbm.1), custom_call_target="tpu_custom_call" | custom-call | tf_op jit(solution)/shard_map/pallas_call | solution.py:371
  123.2 2.3 %copy.9 = f32[512,512]{1,0:T(8,128)} copy(f32[512,512]{1,0:T(8,128)} %shard_map.73) | data formatting | bytes 2097152

commit v2 on v0

v2 whole, which is shorter than its diff:
```python
import functools

import jax
import jax.numpy as jnp
from jax import lax
from jax.experimental import pallas as pl
from jax.experimental.pallas import tpu as pltpu
from jax.sharding import PartitionSpec as P

MESH = pl.DeviceIdType.MESH
NB = 512
HALF = NB // 2
NY, NC, NZ, NX = 4, 2, 8, 4
PART = NB // NX
SUBS = 2
SUB = PART // SUBS
WCH = 4
WCOLS = NB // WCH
RCH = 8
RROWS = HALF // 2
LAG = 2
PAIRED = (0, 1, 4, 5, 8, 9)
RETURNED = (0, 1, 2, 3, 4, 5, 6, 7)
F32 = jnp.float32
BF16 = jnp.bfloat16


def dot1(a, b):
    return jnp.dot(a, b, preferred_element_type=F32)


def split2(a):
    high = a.astype(BF16)
    return high, (a - high.astype(F32)).astype(BF16)


def split3(a):
    high = a.astype(BF16)
    rest = a - high.astype(F32)
    mid = rest.astype(BF16)
    return high, mid, (rest - mid.astype(F32)).astype(BF16)


def product(a, b):
    ah, al = split2(a)
    bh, bl = split2(b)
    return dot1(ah, bh) + (dot1(ah, bl) + dot1(al, bh))


def pick(onehot, parts):
    high, mid, low = parts
    return dot1(onehot, high) + (dot1(onehot, mid) + dot1(onehot, low))


def onehot_of(source, first):
    lanes = lax.broadcasted_iota(jnp.int32, (NB, NB), 1).astype(F32) + first
    return jnp.where(source == lanes, 1.0, 0.0).astype(BF16)


def kernel(
    w_ref, pf_ref, ps_ref, l0_hbm, u0_hbm, l1_hbm, u1_hbm, out_ref,
    l0, u0, l1, u1, xp, sib, hs, turn, mb, xf, xi, px0, px1, c10, c01, ur0, f1,
    gmid, ulmid, bmid, amid, hot, own, moved, fac_sem, sib_s, sib_r,
    p1_s, p1_r, p2f_s, p2f_r, p2b_s, p2b_r, ms_s, ms_r, xs_s, xs_r,
    a_s, a_r, b_s, b_r, c_s, c_r, r_s, r_r, cs_s, cs_r, tmid,
):
    prow = lax.axis_index("prow")
    pcol = lax.axis_index("pcol")
    y, h = prow // 2, prow % 2
    z, x = pcol // NX, pcol % NX
    other = 1 - h
    top = y == 0
    below = y > 0
    row0 = z == 0
    rooted = pcol < 2
    lead = jnp.where(pcol == 0, 1, 0)

    def at(dy=0, dc=0, dz=0, dx=0):
        return {
            "prow": ((y + dy + NY) % NY) * NC + (h + dc) % NC,
            "pcol": ((z + dz + NZ) % NZ) * NX + (x + dx + NX) % NX,
        }

    sibling = at(dc=1)
    pending = []

    def both(*conds):
        conds = [c for c in conds if c is not None]
        return functools.reduce(jnp.logical_and, conds) if conds else None

    def when(cond, fn):
        if cond is None:
            fn()
        else:
            pl.when(cond)(fn)

    def remote(src, dst, ssem, rsem, device):
        return pltpu.make_async_remote_copy(
            src_ref=src, dst_ref=dst, send_sem=ssem, recv_sem=rsem, device_id=device, device_id_type=MESH
        )

    def send(src, dst, ssem, rsem, device, cond=None):
        copy = remote(src, dst, ssem, rsem, device)
        when(cond, copy.start)
        pending.append((cond, copy))

    def await_recv(dst, ssem, rsem, cond=None):
        when(cond, remote(dst, dst, ssem, rsem, sibling).wait_recv)

    factors = [
        pltpu.make_async_copy(src, dst, fac_sem.at[k])
        for k, (src, dst) in enumerate(((l0_hbm, l0), (u0_hbm, u0), (l1_hbm, l1), (u1_hbm, u1)))
    ]
    for copy in factors:
        copy.start()

    partners = [
        at(dc=1), at(dy=1), at(dy=2), at(dy=3), at(dx=1), at(dx=2), at(dx=3),
        at(dz=1), at(dz=2), at(dz=-1), at(dz=-2),
    ]
    barrier = pltpu.get_barrier_semaphore()
    for partner in partners:
        pl.semaphore_signal(barrier, inc=1, device_id=partner, device_id_type=MESH)

    base = (prow * NB).astype(F32)
    chip = (y * 2 * NB).astype(F32)
    pf_row = pf_ref[...].astype(F32)
    ps_row = ps_ref[...].astype(F32)
    row_id = lax.broadcasted_iota(jnp.int32, (NB, NB), 0).astype(F32)
    col_id = lax.broadcasted_iota(jnp.int32, (NB, NB), 1).astype(F32)
    slot_col = row_id[:, 0:1]
    diagonal = row_id == col_id
    pf_col = jnp.sum(jnp.where(diagonal, pf_row, 0.0), axis=1, keepdims=True)
    ps_col = jnp.sum(jnp.where(diagonal, ps_row, 0.0), axis=1, keepdims=True)
    chained = jnp.sum(jnp.where(ps_col == pf_row, col_id + 1.0, 0.0), axis=1, keepdims=True)
    src1 = jnp.where(chained > 0.0, chained - 1.0, ps_col)
    linked_col = jnp.sum(jnp.where(pf_row == row_id + float(NB), col_id + 1.0, 0.0), axis=1, keepdims=True)
    origin_col = jnp.where(linked_col > 0.0, linked_col - 1.0, slot_col + float(NB))
    linked_row = jnp.sum(jnp.where(pf_col == col_id + float(NB), row_id + 1.0, 0.0), axis=0, keepdims=True)
    origin_row = jnp.where(linked_row > 0.0, linked_row, col_id[0:1] + float(NB + 1))
    again = jnp.sum(jnp.where(pf_col == ps_row, origin_row, 0.0), axis=1, keepdims=True)
    back0 = jnp.where(again > 0.0, again - 1.0, slot_col)
    held = float(2 * NB)
    swap0 = jnp.where(jnp.logical_and(top, pf_col >= held), back0, pf_col)
    swap1 = jnp.where(jnp.logical_and(top, src1 >= held), origin_col, src1)
    far = pl.multiple_of(other * HALF, HALF)
    near = pl.multiple_of(h * HALF, HALF)
    wanted = [onehot_of(jnp.where(lead == stage, swap0, swap1), base) for stage in range(2)]
    w_far = split3(w_ref[:, pl.ds(far, HALF)])
    for stage in range(2):
        xp[stage] = pick(wanted[stage], w_far)

    pl.semaphore_wait(barrier, len(partners))

    for c in range(2):
        cols = pl.ds(c * WCOLS, WCOLS)
        for stage in range(2):
            sems = (sib_s.at[c, stage], sib_r.at[c, stage])
            send(xp.at[stage, :, cols], sib.at[stage, :, cols], *sems, sibling)
    w_near = split3(w_ref[:, pl.ds(near, HALF)])
    for stage in range(2):
        hs[stage] = pick(wanted[stage], w_near)

    for stage in range(2):
        source = jnp.where(lead == stage, pf_col, src1)
        inside = jnp.logical_and(source >= chip, source < chip + held)
        own[stage] = jnp.where(inside, 1.0, 0.0)

    def add_other(c):
        cols = pl.ds(c * WCOLS, WCOLS)
        for stage in range(2):
            await_recv(sib.at[stage, :, cols], sib_s.at[c, stage], sib_r.at[c, stage])
            hs[stage, :, cols] = hs[stage, :, cols] + sib[stage, :, cols]

    def piece(way, j):
        s, sub = (j // 2) % 2, j % 2
        rows = pl.ds(way * HALF + sub * RROWS, RROWS)
        cols = pl.ds((j // 4) * WCOLS, WCOLS)
        return s, rows, cols

    ring = {}
    for way in range(2):
        dy = 1 - 2 * way
        first = y == 0
        last = y == (3 if way == 0 else 1)
        between = both(below, jnp.logical_not(last))
        for j in range(RCH):
            where = piece(way, j)
            into = mb.at[(h,) + where]
            done = xf.at[(h,) + where]
            p1 = (p1_s.at[way, j], p1_r.at[way, j])
            copies = dict(
                begin=remote(hs.at[where], into, *p1, at(dy=dy)),
                onward=remote(turn.at[where], into, *p1, at(dy=dy)),
                forth=remote(done, done, p2f_s.at[way, j], p2f_r.at[way, j], at(dy=dy)),
                back=remote(done, done, p2b_s.at[way, j], p2b_r.at[way, j], at(dy=-dy)),
                raw=remote(into, into, ms_s.at[way, j], ms_r.at[way, j], sibling),
                final=remote(done, done, xs_s.at[way, j], xs_r.at[way, j], sibling),
            )
            ring[way, j] = copies
            pending.append((first, copies["begin"]))
            pending.append((between, copies["onward"]))
            pending.append((jnp.logical_or(first, last), copies["forth"]))
            pending.append((last, copies["back"]))
            pending.append((below, copies["raw"]))
            pending.append((None, copies["final"]))

    def first_pass(way, j, hop):
        copies = ring[way, j]
        where = piece(way, j)
        s, rows, cols = where
        copies["onward"].wait_recv()
        copies["raw"].start()
        merged = jnp.where(own[s, rows] > 0.0, hs[where], mb[(h,) + where])
        if hop < NY - 1:
            turn[where] = merged
            copies["onward"].start()
        else:
            xf[(h,) + where] = merged
            copies["forth"].start()
            copies["back"].start()
            copies["final"].start()

    def second_pass(way, j, hop):
        copies = ring[way, j]
        if hop == 2:
            copies["back"].wait_recv()
        else:
            copies["forth"].wait_recv()
        if hop == 0:
            copies["forth"].start()
        copies["final"].start()

    events = {}
    for v in range(NY):
        for way in range(2):
            hop = v if way == 0 else (NY - v) % NY
            for j in range(RCH):
                if hop > 0:
                    events.setdefault((LAG * hop + j, v), []).append((first_pass, way, j, hop))
                if hop < 3:
                    lag = {0: 4, 1: 5, 2: 4}[hop]
                    events.setdefault((LAG * lag + j, v), []).append((second_pass, way, j, hop))

    def slots(begin, end):
        for v in range(NY):
            todo = [e for key in range(begin, end) for e in events.get((key, v), ())]

            def run(todo=todo):
                for fn, way, j, hop in todo:
                    fn(way, j, hop)

            if todo:
                pl.when(y == v)(run)

    def begin_ring(c):
        for j in range(4 * c, 4 * c + 4):
            for way in range(2):
                ring[way, j]["begin"].start()

    def find_rows():
        src1_row = jnp.sum(jnp.where(pf_col == ps_row, row_id + 1.0, 0.0), axis=0, keepdims=True)
        src1_row = jnp.where(src1_row > 0.0, src1_row - 1.0, ps_row)
        count = jnp.zeros((NB, 1), F32)
        for stage in range(2):
            source = jnp.where(lead == stage, pf_row, src1_row)
            mark = jnp.where(source == base + row_id, 1.0, 0.0)
            hot[stage] = mark.astype(BF16)
            count += jnp.sum(mark, axis=1, keepdims=True)
        moved[...] = count

    def place(c):
        for way in range(2):
            for j in range(4 * c, 4 * c + 4):
                ref = mb.at[(other,) + piece(way, j)]
                await_recv(ref, ms_s.at[way, j], ms_r.at[way, j])
        cols = pl.ds(c * WCOLS, WCOLS)
        incoming = jnp.zeros((NB, 2 * WCOLS), F32)
        for stage in range(2):
            rows = jnp.concatenate([mb[0, stage, :, cols], mb[1, stage, :, cols]], axis=1)
            incoming += pick(hot[stage], split3(rows))
        for side in range(2):
            there = pl.ds(side * HALF + c * WCOLS, WCOLS)
            placed = jnp.where(moved[...] > 0.0, incoming[:, side * WCOLS:(side + 1) * WCOLS], w_ref[:, there])
            xi[:, there] = placed

    def place_panel(c):
        @pl.when(both(below, rooted))
        def _():
            place(c)
            for side in range(2):
                there = pl.ds(side * HALF + c * WCOLS, WCOLS)

                @pl.when(pcol == 0)
                def _():
                    px0[:, there] = xi[:, there]

                @pl.when(pcol == 1)
                def _():
                    px1[:, there] = xi[:, there]

    def place_rest(c):
        pl.when(both(below, jnp.logical_not(rooted)))(lambda: place(c))

    def collect_other(stage):
        for way in range(2):
            for j in range(RCH):
                if piece(way, j)[0] == stage:
                    ref = xf.at[(other,) + piece(way, j)]
                    await_recv(ref, xs_s.at[way, j], xs_r.at[way, j])

    units = [(b, s) for s in (0, 2, 1, 3) for b in range(2)] + [(b, s) for b in (2, 3) for s in range(SUBS)]

    def rows_of(unit, part, half=None):
        b, sub = unit
        count = PART if b < 2 else SUB
        first = part * PART + (0 if b < 2 else sub * SUB)
        if half is not None:
            count = count // 2
            first = first + half * count
        rows = pl.ds(pl.multiple_of(first, count), count)
        if b < 2:
            return (px0, px1)[b].at[rows, pl.ds(sub * WCOLS, WCOLS)]
        return (c10, c01)[b - 2].at[h, rows]

    def parts_of(u, column):
        return (column % NX, (column + 2) % NX) if u in PAIRED else (column % NX,)

    def unit_steps(u):
        unit = units[u]
        root = unit[0] % 2
        shared = unit[0] >= 2
        first, later, last = [], [], []

        def put(steps, src, ssem, rsem, device, cond):
            copy = remote(src, src, ssem, rsem, device)
            steps.append((cond, copy.start))
            pending.append((both(None if shared else below, cond), copy))

        def take(steps, ref, ssem, rsem, cond):
            steps.append((cond, remote(ref, ref, ssem, rsem, sibling).wait_recv))

        def across(steps, part, slot):
            ref = rows_of(unit, part)
            sems = (unit[0] - 2, unit[1], slot)
            put(steps, ref, cs_s.at[sems], cs_r.at[sems], sibling, None)

        for d in (1, 3, 2):
            for slot, part in enumerate(parts_of(u, root + d)):
                put(first, rows_of(unit, part), a_s.at[u, slot, d - 1], a_r.at[u, slot], at(dx=d), pcol == root)

        forks = jnp.logical_or(z == 2, z == 6)
        for slot, part in enumerate(parts_of(u, x)):
            ref = rows_of(unit, part)
            take(later, ref, a_s.at[u, slot, 0], a_r.at[u, slot], both(row0, x != root))
            take(later, ref, b_s.at[u, slot, 0], b_r.at[u, slot], z != 0)
            for k, (dz, cond) in enumerate((
                (2, row0), (-2, row0), (1, jnp.logical_or(forks, z == 3)), (-1, forks),
            )):
                put(later, ref, b_s.at[u, slot, k], b_r.at[u, slot], at(dz=dz), cond)
        ref = rows_of(unit, x)
        for d in (1, 3) if u in PAIRED else (1, 3, 2):
            away = z != 0 if u in RETURNED else jnp.logical_not(both(row0, (x + d) % NX == root))
            put(later, ref, c_s.at[u, d - 1], c_r.at[u, d - 1], at(dx=d), away)
        if shared:
            for slot, part in enumerate(parts_of(u, x)):
                across(later, part, 2 * slot)

        for d in (1, 3) if u in PAIRED else (1, 3, 2):
            part = (x + d) % NX
            take(last, rows_of(unit, part), c_s.at[u, 3 - d], c_r.at[u, 3 - d], z != 0 if u in RETURNED else pcol != root)
            pieces = {1: ((None, 1, 0),), 3: ((None, 7, 1),), 2: ((0, 1, 2), (1, 7, 3))}[d]
            for half, level, slot in pieces if u in RETURNED else ():
                ref = rows_of(unit, part, half)
                dz = 1 if level == 7 else -1
                put(last, ref, r_s.at[u, slot], r_r.at[u, slot], at(dz=dz), both(z == level, x != root))
                take(last, ref, r_s.at[u, slot], r_r.at[u, slot], both(row0, x != root))
            if shared:
                across(last, part, d)
        return first, later, last

    steps_of = [unit_steps(u) for u in range(2 * WCH + 2 * SUBS)]

    def carry(phase, chosen, role=None):
        for wanted, plane in ((lambda u: units[u][0] < 2, below), (lambda u: units[u][0] >= 2, None)):
            group = [u for u in chosen if wanted(u)]

            def run(group=group):
                for u in group:
                    for cond, act in steps_of[u][phase]:
                        when(cond, act)

            if group:
                when(both(plane, role), run)

    scatter = functools.partial(carry, 0)
    spread = functools.partial(carry, 1)
    gather = functools.partial(carry, 2)
    is_root = both(row0, rooted)
    is_entry = both(row0, jnp.logical_not(rooted))
    is_fork = jnp.logical_or(z == 2, z == 6)
    is_edge = jnp.logical_or(z == 1, z == 7)
    is_inner = jnp.logical_not(is_edge)
    is_leaf = both(z != 0, jnp.logical_not(is_fork))
    is_far = z != 0

    def spread_own(chosen, mine):
        for column in range(2):
            spread([u for u in chosen if (units[u][0] % 2 == column) == mine], both(row0, pcol == column))

    panel = (tuple(range(0, 4)), tuple(range(4, 8)))
    corner10 = tuple(range(2 * WCH, 2 * WCH + SUBS))
    corner01 = tuple(range(2 * WCH + SUBS, 2 * WCH + 2 * SUBS))
    corners = corner10 + corner01

    def keep_corner(corner):
        corner[h] = xf[h, 0]

    def pivot_rows(q):
        stage = jnp.where(lead == 1, 1 - q, q)
        return jnp.concatenate([xf[0, stage], xf[1, stage]], axis=1)

    for c in range(2):
        add_other(c)
        pl.when(top)(functools.partial(begin_ring, c))
    slots(0, 4)
    pl.when(below)(find_rows)
    slots(4, 6)
    for copy in factors:
        copy.wait()

    @pl.when(below)
    def _():
        gmid[...] = product(u1[...], l1[...])
        ulmid[...] = product(u0[...], l0[...])

    slots(6, 10)
    place_panel(0)
    scatter(panel[0], is_root)
    spread_own(panel[0], True)
    spread(panel[0], is_entry)
    slots(10, 14)
    spread_own(panel[0], False)
    place_panel(1)
    scatter(panel[1], is_root)
    spread_own(panel[1], True)
    spread(panel[0], is_fork)
    slots(14, 16)
    pl.when(pcol == 0)(lambda: keep_corner(c10))
    pl.when(pcol == 1)(lambda: keep_corner(c01))
    scatter(corners, is_root)
    spread_own(corners, True)
    spread_own(panel[1], False)
    spread(panel[1], is_entry)
    spread(panel[0], is_leaf)
    spread_own(corners, False)
    spread(corners, is_entry)
    spread(panel[1], is_fork)
    slots(16, 18)
    place_rest(0)
    spread(panel[1], is_leaf)
    gather(panel[0], is_edge)
    place_rest(1)
    gather(panel[1], is_edge)
    spread(corner10, is_far)
    collect_other(0)

    @pl.when(pcol > 0)
    def _():
        ur0[...] = product(l0[...], pivot_rows(0))

    spread(corner01, is_far)

    @pl.when(pcol > 0)
    def _():
        amid[...] = product(u0[...], ur0[...])

    gather(corners, is_edge)
    gather(panel[0] + panel[1], is_inner)
    def early():
        @pl.when(pcol > 0)
        def _():
            bmid[...] = product(px0[...], ulmid[...])

        @pl.when(pcol > 1)
        def _():
            f1[...] = xi[...] - product(px0[...], amid[...])

    pl.when(below)(early)
    gather(corners, is_inner)

    def whole(ref):
        return jnp.concatenate([ref[0], ref[1]], axis=1)

    def corner_other(b):
        for s in range(SUBS):
            for d in range(NX):
                rows = pl.ds(pl.multiple_of(((x + d) % NX) * PART + s * SUB, SUB), SUB)
                await_recv((c10, c01)[b].at[other, rows], cs_s.at[b, s, d], cs_r.at[b, s, d])

    collect_other(1)
    corner_other(0)

    @pl.when(both(prow > 0, pcol > 0))
    def _():
        right = pivot_rows(1) - product(whole(c10), amid[...])
        tmid[...] = right

        @pl.when(both(below, pcol > 1))
        def _():
            tmid[...] = product(gmid[...], right)

    corner_other(1)
    def first_block():
        @pl.when(pcol == 0)
        def _():
            out_ref[...] = pivot_rows(0)

        @pl.when(pcol > 0)
        def _():
            out_ref[...] = ur0[...]

    def second_block():
        @pl.when(pcol == 0)
        def _():
            out_ref[...] = product(whole(c10), u0[...])

        @pl.when(pcol > 0)
        def _():
            @pl.when(pcol == 1)
            def _():
                out_ref[...] = tmid[...]

            @pl.when(pcol > 1)
            def _():
                out_ref[...] = product(l1[...], tmid[...])

    def trailing():
        @pl.when(pcol == 0)
        def _():
            out_ref[...] = product(px0[...], u0[...])

        @pl.when(pcol > 0)
        def _():
            left = px1[...] - product(bmid[...], whole(c01))

            @pl.when(pcol == 1)
            def _():
                out_ref[...] = product(left, u1[...])

            @pl.when(pcol > 1)
            def _():
                out_ref[...] = f1[...] - product(left, tmid[...])

    pl.when(prow == 0)(first_block)
    pl.when(prow == 1)(second_block)
    pl.when(below)(trailing)

    for cond, copy in pending:
        when(cond, copy.wait_send)


def on_device(
    matrix, pivots_first, pivots_second, lower_first, upper_first, lower_second, upper_second
):
    vmem = pl.BlockSpec(memory_space=pltpu.VMEM)
    anywhere = pl.BlockSpec(memory_space=pl.ANY)
    block = (NB, NB)
    dma = pltpu.SemaphoreType.DMA
    nu = 2 * WCH + 2 * SUBS
    return pl.pallas_call(
        kernel,
        out_shape=jax.ShapeDtypeStruct(block, F32),
        in_specs=[vmem] * 3 + [anywhere] * 4,
        out_specs=vmem,
        scratch_shapes=[pltpu.VMEM(block, F32)] * 4
        + [
            pltpu.VMEM((2, NB, HALF), F32),
            pltpu.VMEM((2, NB, HALF), F32),
            pltpu.VMEM((2, NB, HALF), F32),
            pltpu.VMEM((2, NB, HALF), F32),
            pltpu.VMEM((2, 2, NB, HALF), F32),
            pltpu.VMEM((2, 2, NB, HALF), F32),
            pltpu.VMEM(block, F32),
            pltpu.VMEM(block, F32),
            pltpu.VMEM(block, F32),
            pltpu.VMEM((2, NB, HALF), F32),
            pltpu.VMEM((2, NB, HALF), F32),
        ]
        + [pltpu.VMEM(block, F32)] * 6
        + [pltpu.VMEM((2, NB, NB), BF16), pltpu.VMEM((2, NB, 1), F32), pltpu.VMEM((NB, 1), F32)]
        + [dma((4,)), dma((2, 2)), dma((2, 2))]
        + [dma((2, RCH))] * 10
        + [
            dma((nu, 2, NX - 1)), dma((nu, 2)),
            dma((nu, 2, 4)), dma((nu, 2)),
            dma((nu, NX - 1)), dma((nu, NX - 1)),
            dma((nu, 4)), dma((nu, 4)),
            dma((2, SUBS, NX)), dma((2, SUBS, NX)),
            pltpu.VMEM(block, F32),
        ],
        compiler_params=pltpu.CompilerParams(
            collective_id=0, has_side_effects=True, vmem_limit_bytes=56 << 20
        ),
    )(
        matrix, pivots_first.reshape(1, NB), pivots_second.reshape(1, NB),
        lower_first, upper_first, lower_second, upper_second,
    )


def solution(mesh):
    placed = (P("prow", "pcol"), P(), P(), P(), P(), P(), P())
    return jax.shard_map(
        on_device, mesh=mesh, in_specs=placed, out_specs=P("prow", "pcol"), check_vma=False
    )
```

time: 504 us -> 92.8 us (0.18)
  waiting for transfers between devices: 439 us -> 0 us
  Pallas kernels: 0 us -> 90.4 us
  matrix products: 21.6 us -> 0 us
  local copies, waits for them, and re-layouts: 22.9 us -> 2.26 us
  between operations: 13.3 us -> 0.01 us
  other arithmetic: 5.22 us -> 0 us
    psum x4 -> x0, waiting for transfers between devices: 439 us -> none  [the longest x2 300 us: from_root(): return lax.psum(jnp.where(mine, shard, jnp.zeros_like(shard)), axis)]
    pallas_call x0 -> x1, Pallas kernels: none -> 90.4 us  [on_device(): pl.pallas_call(kernel, out_shape=jax.ShapeDtypeStruct(block, F32), in_spe...]
    dot_general x6 -> x0, matrix products: 21.6 us -> none  [product(): jnp.dot(left, right, precision=lax.Precision.HIGHEST, preferred_element_t...]
    gather x4 -> x0, local copies, waits for them, and re-layouts: 7.79 us -> none  [eliminate(): picked_source = work[pivot_local]]
    scatter x4 -> x0, local copies, waits for them, and re-layouts: 6.15 us -> none  [place_rows(): target_rows = target_rows.at[target].set(old_top, mode='drop')]
    select_n x6 -> x0, other arithmetic: 5.15 us -> none  [the longest x1 2.81 us: from_root(): return lax.psum(jnp.where(mine, shard, jnp.zeros_like(shard)), axis)]
  transfers between devices with their start and end apart: 4 -> 0, of which waited for: 4 -> 0; matrix products, arithmetic and copies ran while one was open for 0% -> 0% of each run, Pallas kernels for 0% -> 0%
where the time goes in v2:
time: 92.8 us; the launch traced here: 92.7 us
  Pallas kernels  90.4 us (97%)
  local copies, waits for them, and re-layouts  2.26 us (2%)
    pallas_call x1, Pallas kernels, on_device(): pl.pallas_call(kernel, out_shape=jax.ShapeDtypeStruct(block, F32), in_spe...  90.4 us
    unnamed x1, local copies, waits for them, and re-layouts  2.26 us

profile of v2, /device:TPU:40, one launch (start us, length us, event | category | flops | bytes accessed | tf_op | source)
XLA Modules:
  0.0 92.7 jit_solution(4231307018919743571)
XLA Ops:
  0.0 90.4 %shard_map.73 = f32[512,512]{1,0:T(8,128)} custom-call(f32[512,512]{1,0:T(8,128)} %w_ref.1, s32[1,512]{1,0:T(1,128)} %bitcast.2, s32[1,512]{1,0:T(1,128)} %bitcast.3, f32[512,512]{1,0:T(8,128)} %l0_hbm.1, f32[512,512]{1,0:T(8,128)} %u0_hbm.1, f32[512,512]{1,0:T(8,128)} %l1_hbm.1, f32[512,512]{1,0:T(8,128)} %u1_hbm.1), custom_call_target="tpu_custom_call" | custom-call | tf_op jit(solution)/shard_map/pallas_call | solution.py:571
  90.4 2.3 %copy.9 = f32[512,512]{1,0:T(8,128)} copy(f32[512,512]{1,0:T(8,128)} %shard_map.73) | data formatting | bytes 2097152

commit v3 on v2

--- a/solution.py
+++ b/solution.py
@@ -19,8 +19,8 @@
 RCH = 8
 RROWS = HALF // 2
 LAG = 2
-PAIRED = (0, 1, 4, 5, 8, 9)
-RETURNED = (0, 1, 2, 3, 4, 5, 6, 7)
+PAIRED = (2, 3, 4, 5, 8, 9, 10, 11)
+RETURNED = (0, 1, 2, 3)
 F32 = jnp.float32
 BF16 = jnp.bfloat16
 
@@ -62,7 +62,7 @@
     l0, u0, l1, u1, xp, sib, hs, turn, mb, xf, xi, px0, px1, c10, c01, ur0, f1,
     gmid, ulmid, bmid, amid, hot, own, moved, fac_sem, sib_s, sib_r,
     p1_s, p1_r, p2f_s, p2f_r, p2b_s, p2b_r, ms_s, ms_r, xs_s, xs_r,
-    a_s, a_r, b_s, b_r, c_s, c_r, r_s, r_r, cs_s, cs_r, tmid,
+    a_s, a_r, b_s, b_r, c_s, c_r, r_s, r_r, y_s, y_r, cs_s, cs_r, tmid, left_near,
 ):
     prow = lax.axis_index("prow")
     pcol = lax.axis_index("pcol")
@@ -94,6 +94,26 @@
         else:
             pl.when(cond)(fn)
 
+    def drain():
+        groups = {}
+        for cond, copy in pending:
+            groups.setdefault(id(cond), (cond, []))[1].append(copy)
+        pending.clear()
+        for cond, copies in groups.values():
+
+            def run(copies=copies):
+                for copy in copies:
+                    copy.wait_send()
+
+            when(cond, run)
+
+    known = {}
+
+    def named(name, make):
+        if name not in known:
+            known[name] = make()
+        return known[name]
+
     def remote(src, dst, ssem, rsem, device):
         return pltpu.make_async_remote_copy(
             src_ref=src, dst_ref=dst, send_sem=ssem, recv_sem=rsem, device_id=device, device_id_type=MESH
@@ -114,13 +134,23 @@
     for copy in factors:
         copy.start()
 
-    partners = [
-        at(dc=1), at(dy=1), at(dy=2), at(dy=3), at(dx=1), at(dx=2), at(dx=3),
-        at(dz=1), at(dz=2), at(dz=-1), at(dz=-2),
-    ]
+    ahead = both(row0, rooted)
+    later = jnp.logical_not(ahead)
+    column = [at(dc=1), at(dy=1), at(dy=2), at(dy=3)]
+    moves = [(0, 1), (0, 2), (0, 3), (1, 0), (2, 0), (-1, 0), (-2, 0)]
+    crosswise = []
+    for dz, dx in moves:
+        theirs = both((z + dz + NZ) % NZ == 0, (x + dx) % NX < 2)
+        crosswise.append((at(dz=dz, dx=dx), theirs))
     barrier = pltpu.get_barrier_semaphore()
-    for partner in partners:
-        pl.semaphore_signal(barrier, inc=1, device_id=partner, device_id_type=MESH)
+
+    def greet(device):
+        pl.semaphore_signal(barrier, inc=1, device_id=device, device_id_type=MESH)
+
+    for device in column:
+        greet(device)
+    for device, theirs in crosswise:
+        pl.when(ahead == theirs)(functools.partial(greet, device))
 
     base = (prow * NB).astype(F32)
     chip = (y * 2 * NB).astype(F32)
@@ -150,7 +180,18 @@
     for stage in range(2):
         xp[stage] = pick(wanted[stage], w_far)
 
-    pl.semaphore_wait(barrier, len(partners))
+    @pl.when(ahead)
+    def _():
+        pl.semaphore_wait(barrier, len(column) + 1)
+        for device, theirs in crosswise:
+            pl.when(jnp.logical_not(theirs))(functools.partial(greet, device))
+
+    @pl.when(later)
+    def _():
+        pl.semaphore_wait(barrier, len(column) + len(crosswise))
+        for device, theirs in crosswise:
+            pl.when(theirs)(functools.partial(greet, device))
+
 
     for c in range(2):
         cols = pl.ds(c * WCOLS, WCOLS)
@@ -184,6 +225,10 @@
         first = y == 0
         last = y == (3 if way == 0 else 1)
         between = both(below, jnp.logical_not(last))
+        whole_ring = jnp.logical_not(rooted)
+        forth_cond = jnp.logical_or(last, both(first, whole_ring))
+        back_cond = both(last, whole_ring)
+        final_cond = jnp.logical_or(top, whole_ring)
         for j in range(RCH):
             where = piece(way, j)
             into = mb.at[(h,) + where]
@@ -200,10 +245,10 @@
             ring[way, j] = copies
             pending.append((first, copies["begin"]))
             pending.append((between, copies["onward"]))
-            pending.append((jnp.logical_or(first, last), copies["forth"]))
-            pending.append((last, copies["back"]))
+            pending.append((forth_cond, copies["forth"]))
+            pending.append((back_cond, copies["back"]))
             pending.append((below, copies["raw"]))
-            pending.append((None, copies["final"]))
+            pending.append((final_cond, copies["final"]))
 
     def first_pass(way, j, hop):
         copies = ring[way, j]
@@ -218,18 +263,27 @@
         else:
             xf[(h,) + where] = merged
             copies["forth"].start()
-            copies["back"].start()
-            copies["final"].start()
+
+            def others():
+                copies["back"].start()
+                copies["final"].start()
+
+            pl.when(jnp.logical_not(rooted))(others)
 
     def second_pass(way, j, hop):
         copies = ring[way, j]
-        if hop == 2:
-            copies["back"].wait_recv()
+        spread_on = jnp.logical_not(rooted)
+        if hop == 0:
+            copies["forth"].wait_recv()
+            when(spread_on, copies["forth"].start)
+            copies["final"].start()
         else:
-            copies["forth"].wait_recv()
-        if hop == 0:
-            copies["forth"].start()
-        copies["final"].start()
+
+            def arrive():
+                copies["back" if hop == 2 else "forth"].wait_recv()
+                copies["final"].start()
+
+            when(spread_on, arrive)
 
     events = {}
     for v in range(NY):
@@ -311,6 +365,10 @@
 
     units = [(b, s) for s in (0, 2, 1, 3) for b in range(2)] + [(b, s) for b in (2, 3) for s in range(SUBS)]
 
+    corner10 = tuple(range(2 * WCH, 2 * WCH + SUBS))
+    corner01 = tuple(range(2 * WCH + SUBS, 2 * WCH + 2 * SUBS))
+    corners = corner10 + corner01
+
     def rows_of(unit, part, half=None):
         b, sub = unit
         count = PART if b < 2 else SUB
@@ -326,6 +384,19 @@
     def parts_of(u, column):
         return (column % NX, (column + 2) % NX) if u in PAIRED else (column % NX,)
 
+    tests = {
+        None: None, "row0": row0, "far": z != 0, "forks": jnp.logical_or(z == 2, z == 6),
+        "rise": jnp.logical_or(jnp.logical_or(z == 2, z == 6), z == 3),
+    }
+    for root in range(2):
+        tests["root", root] = pcol == root
+        tests["apart", root] = pcol != root
+        tests["enter", root] = both(row0, x != root)
+        for level in (1, 7):
+            tests["edge", root, level] = both(z == level, x != root)
+        for d in range(1, NX):
+            tests["away", root, d] = jnp.logical_not(both(row0, (x + d) % NX == root))
+
     def unit_steps(u):
         unit = units[u]
         root = unit[0] % 2
@@ -335,7 +406,8 @@
         def put(steps, src, ssem, rsem, device, cond):
             copy = remote(src, src, ssem, rsem, device)
             steps.append((cond, copy.start))
-            pending.append((both(None if shared else below, cond), copy))
+            whole = named((shared, cond), lambda: both(top if shared else below, tests[cond]))
+            pending.append((whole, copy))
 
         def take(steps, ref, ssem, rsem, cond):
             steps.append((cond, remote(ref, ref, ssem, rsem, sibling).wait_recv))
@@ -344,23 +416,23 @@
             ref = rows_of(unit, part)
             sems = (unit[0] - 2, unit[1], slot)
             put(steps, ref, cs_s.at[sems], cs_r.at[sems], sibling, None)
+            put(steps, ref, y_s.at[sems], y_r.at[sems], at(dy=1 if slot < 2 else -1), None)
 
         for d in (1, 3, 2):
             for slot, part in enumerate(parts_of(u, root + d)):
-                put(first, rows_of(unit, part), a_s.at[u, slot, d - 1], a_r.at[u, slot], at(dx=d), pcol == root)
-
-        forks = jnp.logical_or(z == 2, z == 6)
+                put(first, rows_of(unit, part), a_s.at[u, slot, d - 1], a_r.at[u, slot], at(dx=d), ("root", root))
+
         for slot, part in enumerate(parts_of(u, x)):
             ref = rows_of(unit, part)
-            take(later, ref, a_s.at[u, slot, 0], a_r.at[u, slot], both(row0, x != root))
-            take(later, ref, b_s.at[u, slot, 0], b_r.at[u, slot], z != 0)
+            take(later, ref, a_s.at[u, slot, 0], a_r.at[u, slot], ("enter", root))
+            take(later, ref, b_s.at[u, slot, 0], b_r.at[u, slot], "far")
             for k, (dz, cond) in enumerate((
-                (2, row0), (-2, row0), (1, jnp.logical_or(forks, z == 3)), (-1, forks),
+                (2, "row0"), (-2, "row0"), (1, "rise"), (-1, "forks"),
             )):
                 put(later, ref, b_s.at[u, slot, k], b_r.at[u, slot], at(dz=dz), cond)
         ref = rows_of(unit, x)
         for d in (1, 3) if u in PAIRED else (1, 3, 2):
-            away = z != 0 if u in RETURNED else jnp.logical_not(both(row0, (x + d) % NX == root))
+            away = "far" if u in RETURNED else ("away", root, d)
             put(later, ref, c_s.at[u, d - 1], c_r.at[u, d - 1], at(dx=d), away)
         if shared:
             for slot, part in enumerate(parts_of(u, x)):
@@ -368,13 +440,13 @@
 
         for d in (1, 3) if u in PAIRED else (1, 3, 2):
             part = (x + d) % NX
-            take(last, rows_of(unit, part), c_s.at[u, 3 - d], c_r.at[u, 3 - d], z != 0 if u in RETURNED else pcol != root)
+            take(last, rows_of(unit, part), c_s.at[u, 3 - d], c_r.at[u, 3 - d], "far" if u in RETURNED else ("apart", root))
             pieces = {1: ((None, 1, 0),), 3: ((None, 7, 1),), 2: ((0, 1, 2), (1, 7, 3))}[d]
             for half, level, slot in pieces if u in RETURNED else ():
                 ref = rows_of(unit, part, half)
                 dz = 1 if level == 7 else -1
-                put(last, ref, r_s.at[u, slot], r_r.at[u, slot], at(dz=dz), both(z == level, x != root))
-                take(last, ref, r_s.at[u, slot], r_r.at[u, slot], both(row0, x != root))
+                put(last, ref, r_s.at[u, slot], r_r.at[u, slot], at(dz=dz), ("edge", root, level))
+                take(last, ref, r_s.at[u, slot], r_r.at[u, slot], ("enter", root))
             if shared:
                 across(last, part, d)
         return first, later, last
@@ -382,13 +454,19 @@
     steps_of = [unit_steps(u) for u in range(2 * WCH + 2 * SUBS)]
 
     def carry(phase, chosen, role=None):
-        for wanted, plane in ((lambda u: units[u][0] < 2, below), (lambda u: units[u][0] >= 2, None)):
+        for wanted, plane in ((lambda u: units[u][0] < 2, below), (lambda u: units[u][0] >= 2, top)):
             group = [u for u in chosen if wanted(u)]
 
             def run(group=group):
+                merged = []
                 for u in group:
                     for cond, act in steps_of[u][phase]:
-                        when(cond, act)
+                        if merged and merged[-1][0] == cond:
+                            merged[-1][1].append(act)
+                        else:
+                            merged.append((cond, [act]))
+                for cond, acts in merged:
+                    when(tests[cond], lambda acts=acts: [act() for act in acts] and None)
 
             if group:
                 when(both(plane, role), run)
@@ -404,14 +482,52 @@
     is_leaf = both(z != 0, jnp.logical_not(is_fork))
     is_far = z != 0
 
+    handed = {}
+    late = []
+    for u in corners:
+        b, s = units[u][0] - 2, units[u][1]
+        for slot in range(NX):
+            ref = rows_of(units[u], (x + slot) % NX)
+            sems = (b, s, slot)
+            onward = remote(ref, ref, y_s.at[sems], y_r.at[sems], at(dy=1 if slot < 2 else -1))
+            across = remote(ref, ref, cs_s.at[sems], cs_r.at[sems], sibling)
+            handed[u, slot] = onward, across
+            middle = named(("middle", slot < 2), lambda: jnp.logical_or(y == 2, y == (1 if slot < 2 else 3)))
+            late.append((middle, onward))
+            late.append((below, across))
+
+    def hand_down(stage):
+        for v in range(1, NY):
+            near, away = ((2, 3), (0, 1)) if v == 3 else ((0, 1), (2, 3))
+            if v == 2:
+                todo = (
+                    [(u, slot) for u in corners for slot in (0, 2)],
+                    [(u, slot) for u in corners for slot in (1, 3)],
+                    [],
+                )[stage]
+            else:
+                todo = (
+                    [(u, near[0]) for u in corners],
+                    [(u, near[1]) for u in corners],
+                    [(u, slot) for slot in away for u in corners],
+                )[stage]
+
+            def run(todo=todo, v=v):
+                for u, slot in todo:
+                    onward, across = handed[u, slot]
+                    onward.wait_recv()
+                    if v == 2 or v == (1 if slot < 2 else 3):
+                        onward.start()
+                    across.start()
+
+            if todo:
+                pl.when(y == v)(run)
+
     def spread_own(chosen, mine):
         for column in range(2):
             spread([u for u in chosen if (units[u][0] % 2 == column) == mine], both(row0, pcol == column))
 
     panel = (tuple(range(0, 4)), tuple(range(4, 8)))
-    corner10 = tuple(range(2 * WCH, 2 * WCH + SUBS))
-    corner01 = tuple(range(2 * WCH + SUBS, 2 * WCH + 2 * SUBS))
-    corners = corner10 + corner01
 
     def keep_corner(corner):
         corner[h] = xf[h, 0]
@@ -436,6 +552,7 @@
 
     slots(6, 10)
     place_panel(0)
+    pl.when(ahead)(lambda: pl.semaphore_wait(barrier, len(crosswise) - 1))
     scatter(panel[0], is_root)
     spread_own(panel[0], True)
     spread(panel[0], is_entry)
@@ -446,8 +563,8 @@
     spread_own(panel[1], True)
     spread(panel[0], is_fork)
     slots(14, 16)
-    pl.when(pcol == 0)(lambda: keep_corner(c10))
-    pl.when(pcol == 1)(lambda: keep_corner(c01))
+    pl.when(both(top, pcol == 0))(lambda: keep_corner(c10))
+    pl.when(both(top, pcol == 1))(lambda: keep_corner(c01))
     scatter(corners, is_root)
     spread_own(corners, True)
     spread_own(panel[1], False)
@@ -459,24 +576,24 @@
     slots(16, 18)
     place_rest(0)
     spread(panel[1], is_leaf)
+    spread(corner10, is_far)
+    spread(corner01, is_far)
+    gather(corner10)
+    gather(corner01)
     gather(panel[0], is_edge)
     place_rest(1)
-    gather(panel[1], is_edge)
-    spread(corner10, is_far)
-    collect_other(0)
-
-    @pl.when(pcol > 0)
+    hand_down(0)
+    hand_down(1)
+    apart = jnp.logical_or(top, jnp.logical_not(rooted))
+    pl.when(apart)(lambda: collect_other(0))
+
+    @pl.when(both(pcol > 0, apart))
     def _():
         ur0[...] = product(l0[...], pivot_rows(0))
-
-    spread(corner01, is_far)
-
-    @pl.when(pcol > 0)
-    def _():
         amid[...] = product(u0[...], ur0[...])
 
-    gather(corners, is_edge)
-    gather(panel[0] + panel[1], is_inner)
+    gather(panel[0], is_inner)
+    gather(panel[1])
     def early():
         @pl.when(pcol > 0)
         def _():
@@ -487,7 +604,8 @@
             f1[...] = xi[...] - product(px0[...], amid[...])
 
     pl.when(below)(early)
-    gather(corners, is_inner)
+    drain()
+    hand_down(2)
 
     def whole(ref):
         return jnp.concatenate([ref[0], ref[1]], axis=1)
@@ -498,10 +616,10 @@
                 rows = pl.ds(pl.multiple_of(((x + d) % NX) * PART + s * SUB, SUB), SUB)
                 await_recv((c10, c01)[b].at[other, rows], cs_s.at[b, s, d], cs_r.at[b, s, d])
 
-    collect_other(1)
+    pl.when(apart)(lambda: collect_other(1))
     corner_other(0)
 
-    @pl.when(both(prow > 0, pcol > 0))
+    @pl.when(both(prow > 0, jnp.logical_or(pcol > 1, both(top, pcol == 1))))
     def _():
         right = pivot_rows(1) - product(whole(c10), amid[...])
         tmid[...] = right
@@ -510,6 +628,15 @@
         def _():
             tmid[...] = product(gmid[...], right)
 
+
+    @pl.when(both(below, pcol > 0))
+    def _():
+        left_near[...] = px1[:, pl.ds(near, HALF)] - product(bmid[...], c01[h])
+
+        @pl.when(pcol > 1)
+        def _():
+            f1[...] = f1[...] - product(left_near[...], tmid[pl.ds(near, HALF)])
+
     corner_other(1)
     def first_block():
         @pl.when(pcol == 0)
@@ -542,22 +669,22 @@
 
         @pl.when(pcol > 0)
         def _():
-            left = px1[...] - product(bmid[...], whole(c01))
+            left_far = px1[:, pl.ds(far, HALF)] - product(bmid[...], c01[other])
 
             @pl.when(pcol == 1)
             def _():
-                out_ref[...] = product(left, u1[...])
+                out_ref[...] = product(left_near[...], u1[pl.ds(near, HALF)]) + product(left_far, u1[pl.ds(far, HALF)])
 
             @pl.when(pcol > 1)
             def _():
-                out_ref[...] = f1[...] - product(left, tmid[...])
+                out_ref[...] = f1[...] - product(left_far, tmid[pl.ds(far, HALF)])
 
     pl.when(prow == 0)(first_block)
     pl.when(prow == 1)(second_block)
     pl.when(below)(trailing)
 
-    for cond, copy in pending:
-        when(cond, copy.wait_send)
+    pending.extend(late)
+    drain()
 
 
 def on_device(
@@ -597,7 +724,9 @@
             dma((nu, NX - 1)), dma((nu, NX - 1)),
             dma((nu, 4)), dma((nu, 4)),
             dma((2, SUBS, NX)), dma((2, SUBS, NX)),
+            dma((2, SUBS, NX)), dma((2, SUBS, NX)),
             pltpu.VMEM(block, F32),
+            pltpu.VMEM((NB, HALF), F32),
         ],
         compiler_params=pltpu.CompilerParams(
             collective_id=0, has_side_effects=True, vmem_limit_bytes=56 << 20

time: 92.8 us -> 88.2 us (0.950)
  the two profiles are of different devices: /device:TPU:40 before, /device:TPU:144 now
where the time goes in v3:
time: 88.2 us; the launch traced here: 88.1 us
  Pallas kernels  85.8 us (97%)
  local copies, waits for them, and re-layouts  2.26 us (3%)
    pallas_call x1, Pallas kernels, on_device(): pl.pallas_call(kernel, out_shape=jax.ShapeDtypeStruct(block, F32), in_spe...  85.8 us
    unnamed x1, local copies, waits for them, and re-layouts  2.26 us

profile of v3, /device:TPU:144, one launch (start us, length us, event | category | flops | bytes accessed | tf_op | source)
XLA Modules:
  0.0 88.1 jit_solution(474320391152282340)
XLA Ops:
  0.0 85.8 %shard_map.73 = f32[512,512]{1,0:T(8,128)} custom-call(f32[512,512]{1,0:T(8,128)} %w_ref.1, s32[1,512]{1,0:T(1,128)} %bitcast.2, s32[1,512]{1,0:T(1,128)} %bitcast.3, f32[512,512]{1,0:T(8,128)} %l0_hbm.1, f32[512,512]{1,0:T(8,128)} %u0_hbm.1, f32[512,512]{1,0:T(8,128)} %l1_hbm.1, f32[512,512]{1,0:T(8,128)} %u1_hbm.1), custom_call_target="tpu_custom_call" | custom-call | tf_op jit(solution)/shard_map/pallas_call | solution.py:698
  85.8 2.3 %copy.9 = f32[512,512]{1,0:T(8,128)} copy(f32[512,512]{1,0:T(8,128)} %shard_map.73) | data formatting | bytes 2097152

commit v4 on v3

--- a/solution.py
+++ b/solution.py
@@ -41,10 +41,22 @@
     return high, mid, (rest - mid.astype(F32)).astype(BF16)
 
 
+def joined(a, b):
+    ah, al = a
+    bh, bl = b
+    return dot1(ah, bh) + (dot1(ah, bl) + dot1(al, bh))
+
+
 def product(a, b):
-    ah, al = split2(a)
-    bh, bl = split2(b)
-    return dot1(ah, bh) + (dot1(ah, bl) + dot1(al, bh))
+    return joined(split2(a), split2(b))
+
+
+def keep(ref, value):
+    ref[0], ref[1] = split2(value)
+
+
+def both_parts(ref):
+    return ref[0], ref[1]
 
 
 def pick(onehot, parts):
@@ -58,8 +70,8 @@
 
 
 def kernel(
-    w_ref, pf_ref, ps_ref, l0_hbm, u0_hbm, l1_hbm, u1_hbm, out_ref,
-    l0, u0, l1, u1, xp, sib, hs, turn, mb, xf, xi, px0, px1, c10, c01, ur0, f1,
+    w_hbm, pf_ref, ps_ref, l0_hbm, u0_hbm, l1_hbm, u1_hbm, out_ref,
+    w_ref, l0, u0, l1, u1, xp, sib, hs, turn, mb, xf, xi, px0, px1, c10, c01, ur0, f1,
     gmid, ulmid, bmid, amid, hot, own, moved, fac_sem, sib_s, sib_r,
     p1_s, p1_r, p2f_s, p2f_r, p2b_s, p2b_r, ms_s, ms_r, xs_s, xs_r,
     a_s, a_r, b_s, b_r, c_s, c_r, r_s, r_r, y_s, y_r, cs_s, cs_r, tmid, left_near,
@@ -127,6 +139,8 @@
     def await_recv(dst, ssem, rsem, cond=None):
         when(cond, remote(dst, dst, ssem, rsem, sibling).wait_recv)
 
+    load = pltpu.make_async_copy(w_hbm, w_ref, fac_sem.at[4])
+    load.start()
     factors = [
         pltpu.make_async_copy(src, dst, fac_sem.at[k])
         for k, (src, dst) in enumerate(((l0_hbm, l0), (u0_hbm, u0), (l1_hbm, l1), (u1_hbm, u1)))
@@ -176,6 +190,7 @@
     far = pl.multiple_of(other * HALF, HALF)
     near = pl.multiple_of(h * HALF, HALF)
     wanted = [onehot_of(jnp.where(lead == stage, swap0, swap1), base) for stage in range(2)]
+    load.wait()
     w_far = split3(w_ref[:, pl.ds(far, HALF)])
     for stage in range(2):
         xp[stage] = pick(wanted[stage], w_far)
@@ -509,7 +524,7 @@
                 todo = (
                     [(u, near[0]) for u in corners],
                     [(u, near[1]) for u in corners],
-                    [(u, slot) for slot in away for u in corners],
+                    [(u, slot) for b in (corner10, corner01) for slot in away for u in b],
                 )[stage]
 
             def run(todo=todo, v=v):
@@ -545,10 +560,10 @@
     for copy in factors:
         copy.wait()
 
-    @pl.when(below)
+    @pl.when(both(below, jnp.logical_not(rooted)))
     def _():
-        gmid[...] = product(u1[...], l1[...])
-        ulmid[...] = product(u0[...], l0[...])
+        keep(gmid, product(u1[...], l1[...]))
+        keep(ulmid, product(u0[...], l0[...]))
 
     slots(6, 10)
     place_panel(0)
@@ -581,8 +596,8 @@
     gather(corner10)
     gather(corner01)
     gather(panel[0], is_edge)
+    hand_down(0)
     place_rest(1)
-    hand_down(0)
     hand_down(1)
     apart = jnp.logical_or(top, jnp.logical_not(rooted))
     pl.when(apart)(lambda: collect_other(0))
@@ -590,18 +605,23 @@
     @pl.when(both(pcol > 0, apart))
     def _():
         ur0[...] = product(l0[...], pivot_rows(0))
-        amid[...] = product(u0[...], ur0[...])
+        keep(amid, product(u0[...], ur0[...]))
 
     gather(panel[0], is_inner)
     gather(panel[1])
     def early():
         @pl.when(pcol > 0)
         def _():
-            bmid[...] = product(px0[...], ulmid[...])
-
-        @pl.when(pcol > 1)
-        def _():
-            f1[...] = xi[...] - product(px0[...], amid[...])
+            @pl.when(pcol == 1)
+            def _():
+                keep(ulmid, product(u0[...], l0[...]))
+
+            panel_parts = split2(px0[...])
+            keep(bmid, joined(panel_parts, both_parts(ulmid)))
+
+            @pl.when(pcol > 1)
+            def _():
+                f1[...] = xi[...] - joined(panel_parts, both_parts(amid))
 
     pl.when(below)(early)
     drain()
@@ -621,17 +641,17 @@
 
     @pl.when(both(prow > 0, jnp.logical_or(pcol > 1, both(top, pcol == 1))))
     def _():
-        right = pivot_rows(1) - product(whole(c10), amid[...])
+        right = pivot_rows(1) - joined(split2(whole(c10)), both_parts(amid))
         tmid[...] = right
 
         @pl.when(both(below, pcol > 1))
         def _():
-            tmid[...] = product(gmid[...], right)
+            tmid[...] = joined(both_parts(gmid), split2(right))
 
 
     @pl.when(both(below, pcol > 0))
     def _():
-        left_near[...] = px1[:, pl.ds(near, HALF)] - product(bmid[...], c01[h])
+        left_near[...] = px1[:, pl.ds(near, HALF)] - joined(both_parts(bmid), split2(c01[h]))
 
         @pl.when(pcol > 1)
         def _():
@@ -669,7 +689,7 @@
 
         @pl.when(pcol > 0)
         def _():
-            left_far = px1[:, pl.ds(far, HALF)] - product(bmid[...], c01[other])
+            left_far = px1[:, pl.ds(far, HALF)] - joined(both_parts(bmid), split2(c01[other]))
 
             @pl.when(pcol == 1)
             def _():
@@ -698,9 +718,9 @@
     return pl.pallas_call(
         kernel,
         out_shape=jax.ShapeDtypeStruct(block, F32),
-        in_specs=[vmem] * 3 + [anywhere] * 4,
+        in_specs=[anywhere] + [vmem] * 2 + [anywhere] * 4,
         out_specs=vmem,
-        scratch_shapes=[pltpu.VMEM(block, F32)] * 4
+        scratch_shapes=[pltpu.VMEM(block, F32)] * 5
         + [
             pltpu.VMEM((2, NB, HALF), F32),
             pltpu.VMEM((2, NB, HALF), F32),
@@ -714,9 +734,10 @@
             pltpu.VMEM((2, NB, HALF), F32),
             pltpu.VMEM((2, NB, HALF), F32),
         ]
-        + [pltpu.VMEM(block, F32)] * 6
-        + [pltpu.VMEM((2, NB, NB), BF16), pltpu.VMEM((2, NB, 1), F32), pltpu.VMEM((NB, 1), F32)]
-        + [dma((4,)), dma((2, 2)), dma((2, 2))]
+        + [pltpu.VMEM(block, F32)] * 2
+        + [pltpu.VMEM((2, NB, NB), BF16)] * 5
+        + [pltpu.VMEM((2, NB, 1), F32), pltpu.VMEM((NB, 1), F32)]
+        + [dma((5,)), dma((2, 2)), dma((2, 2))]
         + [dma((2, RCH))] * 10
         + [
             dma((nu, 2, NX - 1)), dma((nu, 2)),

time: 88.2 us -> 86.2 us (0.977)
  the two profiles are of different devices: /device:TPU:144 before, /device:TPU:40 now
where the time goes in v4:
time: 86.2 us; the launch traced here: 84.5 us
  Pallas kernels  82.2 us (95%)
  local copies, waits for them, and re-layouts  2.26 us (3%)
    pallas_call x1, Pallas kernels, on_device(): pl.pallas_call(kernel, out_shape=jax.ShapeDtypeStruct(block, F32), in_spe...  82.2 us
    unnamed x1, local copies, waits for them, and re-layouts  2.26 us

profile of v4, /device:TPU:40, one launch (start us, length us, event | category | flops | bytes accessed | tf_op | source)
XLA Modules:
  0.0 84.5 jit_solution(2195571108191431895)
XLA Ops:
  0.0 82.2 %shard_map.73 = f32[512,512]{1,0:T(8,128)} custom-call(f32[512,512]{1,0:T(8,128)} %w_hbm.1, s32[1,512]{1,0:T(1,128)} %bitcast.2, s32[1,512]{1,0:T(1,128)} %bitcast.3, f32[512,512]{1,0:T(8,128)} %l0_hbm.1, f32[512,512]{1,0:T(8,128)} %u0_hbm.1, f32[512,512]{1,0:T(8,128)} %l1_hbm.1, f32[512,512]{1,0:T(8,128)} %u1_hbm.1), custom_call_target="tpu_custom_call" | custom-call | tf_op jit(solution)/shard_map/pallas_call | solution.py:718
  82.2 2.3 %copy.9 = f32[512,512]{1,0:T(8,128)} copy(f32[512,512]{1,0:T(8,128)} %shard_map.73) | data formatting | bytes 2097152
